TPU v7x, 512 devices: a whole 4x4x16 slice. The times are simulated.
512 devices in a mesh: view: 4 (over x_hi, core), brick: 128 (over z, y, x_lo).
Axes of the slice: x: 4 (x_hi: 2, x_lo: 2; x = x_hi * 2 + x_lo), y: 4, z: 16, core: 2. Of those that a mesh axis runs over, the one named last changes fastest.
Arguments:
- estimate: float32 [128, 2048, 128], P('brick'), may hold values from 0.5 to 2
- observed: float32 [4, 128, 2048, 128], P('view', None, 'brick'), may hold values from 0.25 to 4
- long_taps: float32 [4, 31], P('view'), may hold values from 0.05 to 1
- short_taps: float32 [4, 2, 7], P('view'), may hold values from 0.05 to 1
- brick_map: int32 [4, 128], P('view'), may hold values from 0 to 127, each once within a row
- valid_rows: int32 [4, 128], P('view'), may hold values from 512 to 2048
Outputs:
- refined: float32 [128, 2048, 128], P('brick')
Inputs may be any that keep to these rules, and one draw needn't show every extreme that they name: Each view's row of brick_map names every reference brick exactly once.
All inputs are finite; a program needn't handle non-finite values.
Results may differ from a plain program's by a relative error of at most 0.0001.
Values sent between devices are 32-bit elements; how exact they have to be, the bound alone decides.
A program may use at most 64 MiB of HBM per device.

v0:
```python
import jax
import jax.numpy as jnp
from jax import lax
from jax.sharding import PartitionSpec as P

ITERS = 2


def with_halo(block, sides, width):
    for axis, dim in sides:
        count = lax.axis_size(axis)
        forward = [(i, i + 1) for i in range(count - 1)]
        backward = [(target, source) for source, target in forward]
        low = lax.ppermute(
            lax.slice_in_dim(block, block.shape[dim] - width, None, axis=dim), axis, forward
        )
        high = lax.ppermute(lax.slice_in_dim(block, 0, width, axis=dim), axis, backward)
        block = jnp.concatenate([low, block, high], axis=dim)
    return block


def blur_axis(volume, kernel, dimension, adjoint):
    kernel_size = kernel.shape[0]
    radius = kernel_size // 2
    if adjoint:
        kernel = kernel[::-1]
    padding = [(0, 0)] * 3
    padding[dimension] = (radius, radius)
    padded = jnp.pad(volume, padding)
    length = volume.shape[dimension]
    summed = jnp.zeros(volume.shape, jnp.float32)
    for offset in range(kernel_size):
        summed = summed + kernel[offset] * lax.slice_in_dim(
            padded, offset, offset + length, axis=dimension
        )
    return summed


def blur_rows(volume, kernel, adjoint):
    kernel_size = kernel.shape[0]
    radius = kernel_size // 2
    if adjoint:
        kernel = kernel[::-1]
    padded = with_halo(volume, (("brick", 1),), radius)
    length = volume.shape[1]
    summed = jnp.zeros(volume.shape, jnp.float32)
    for offset in range(kernel_size):
        summed = summed + kernel[offset] * lax.slice_in_dim(padded, offset, offset + length, axis=1)
    return summed


def to_view(volume, forward_map):
    arrived = lax.all_to_all(volume, "brick", split_axis=1, concat_axis=0, tiled=True)
    brick_count = forward_map.shape[0]
    bricks = arrived.reshape(brick_count, -1, arrived.shape[1], arrived.shape[2])
    return bricks[forward_map].reshape(arrived.shape)


def to_reference(volume, inverse):
    brick_count = inverse.shape[0]
    bricks = volume.reshape(brick_count, -1, volume.shape[1], volume.shape[2])
    ordered = bricks[inverse].reshape(volume.shape)
    return lax.all_to_all(ordered, "brick", split_axis=0, concat_axis=1, tiled=True)


def on_device(estimate, observed, long_taps, short_taps, brick_map, valid_rows):
    kernel_long = long_taps[0] / jnp.sum(long_taps[0])
    kernel_plane = short_taps[0, 0] / jnp.sum(short_taps[0, 0])
    kernel_column = short_taps[0, 1] / jnp.sum(short_taps[0, 1])
    forward_map = brick_map[0]
    inverse = jnp.argsort(forward_map)
    observed_view = observed[0]
    row_count = observed_view.shape[1]
    row_ids = lax.axis_index("brick") * row_count + jnp.arange(row_count, dtype=jnp.int32)
    limits = jnp.repeat(valid_rows[0], observed_view.shape[0] // forward_map.shape[0])
    valid_mask = (row_ids[None, :] < limits[:, None])[:, :, None]
    current = estimate
    for iteration in range(ITERS):
        framed = to_view(current, forward_map)
        blurred = blur_rows(framed, kernel_long, False)
        blurred = blur_axis(blur_axis(blurred, kernel_plane, 0, False), kernel_column, 2, False)
        ratios = jnp.where(valid_mask, observed_view / blurred, 1.0)
        spread_back = blur_axis(blur_axis(ratios, kernel_plane, 0, True), kernel_column, 2, True)
        correction = to_reference(blur_rows(spread_back, kernel_long, True), inverse)
        log_terms = jnp.log(correction)
        current = current * jnp.exp(lax.psum(log_terms, "view"))
    return current


def solution(mesh):
    placed = (
        P("brick", None, None),
        P("view", None, "brick", None),
        P("view", None),
        P("view", None, None),
        P("view", None),
        P("view", None),
    )
    return jax.shard_map(
        on_device, mesh=mesh, in_specs=placed, out_specs=P("brick", None, None), check_vma=False
    )
```

profile of v0, /device:TPU:1, one launch (start us, length us, event | category | flops | bytes accessed | tf_op | source)
XLA Modules:
  0.0 746.9 jit_solution(6758244654196915608)
XLA Ops:
  6.5 21.6 %all-to-all-start = ((f32[1,2048,128]{2,0,1:T(1,128)}), f32[1,2048,128]{2,0,1:T(1,128)S(1)}, u32[]{:S(2)}, u32[]{:S(2)}) async-start(f32[1,2048,128]{2,0,1:T(1,128)} %bitcast.120), calls=%async_computation | async-start | bytes 2097152 | tf_op jit(solution)/shard_map/all_to_all | solution.py:53
  33.7 43.9 %all-to-all-done = f32[1,2048,128]{2,0,1:T(1,128)S(1)} async-done(((f32[1,2048,128]{2,0,1:T(1,128)}), f32[1,2048,128]{2,0,1:T(1,128)S(1)}, u32[]{:S(2)}, u32[]{:S(2)}) %all-to-all-start) | async-done | bytes 1048608 | tf_op jit(solution)/shard_map/all_to_all | solution.py:53
  86.4 33.4 %collective-permute-done = f32[128,15,128]{2,0,1:T(8,128)S(1)} collective-permute-done((f32[128,15,128]{2,0,1:T(8,128)S(1)}, f32[128,15,128]{2,0,1:T(8,128)S(1)}, u32[]{:S(2)}, u32[]{:S(2)}) %collective-permute-start) | collective-permute-done | bytes 983072 | tf_op jit(solution)/shard_map/ppermute | solution.py:14
  121.0 24.0 %fusion.299 = f32[128,16,128]{2,1,0:T(8,128)S(1)} fusion(f32[128,15,128]{2,1,0:T(8,128)S(1)} %copy.13, f32[128,16,128]{2,1,0:T(8,128)S(1)} %gather_fusion, f32[128,31,128]{2,1,0:T(8,128)S(1)} %copy_dynamic-update-slice_fusion.1, f32[]{:T(128)} %bitcast.44, f32[]{:T(128)} %bitcast.43, f32[]{:T(128)} %bitcast.42, f32[]{:T(128)} %bitcast.41, f32[]{:T(128)} %bitcast.40, ...), kind=kLoop, calls=%fused_computation.495 | loop fusion | flops 19922944 | bytes 18808956 | tf_op jit(solution)/shard_map/add | solution.py:48
  145.0 4.9 multiply_add_fusion.3
  149.9 6.3 fusion.357
  161.1 6.1 fusion.19
  171.2 5.9 collective-permute-start.2
  181.2 9.6 %collective-permute-done.3 = f32[128,15,128]{2,0,1:T(8,128)} collective-permute-done((f32[128,15,128]{2,0,1:T(8,128)}, f32[128,15,128]{2,0,1:T(8,128)}, u32[]{:S(2)}, u32[]{:S(2)}) %collective-permute-start.3) | collective-permute-done | bytes 983072 | tf_op jit(solution)/shard_map/ppermute | solution.py:17
  192.6 26.0 %collective-permute-done.2 = f32[128,15,128]{2,0,1:T(8,128)S(1)} collective-permute-done((f32[128,15,128]{2,0,1:T(8,128)}, f32[128,15,128]{2,0,1:T(8,128)S(1)}, u32[]{:S(2)}, u32[]{:S(2)}) %collective-permute-start.2) | collective-permute-done | bytes 983072 | tf_op jit(solution)/shard_map/ppermute | solution.py:14
  219.1 25.1 %fusion.197 = f32[128,16,128]{2,1,0:T(8,128)S(1)} fusion(f32[128,16,128]{2,1,0:T(8,128)S(1)} %fusion.19, f32[128,15,128]{2,1,0:T(8,128)S(1)} %copy.19, f32[128,15,128]{2,1,0:T(8,128)S(1)} %copy.17, f32[]{:T(128)} %bitcast.98, f32[]{:T(128)} %bitcast.97, f32[]{:T(128)} %bitcast.96, f32[]{:T(128)} %bitcast.95, f32[]{:T(128)} %bitcast.94, f32[]{:T(128)} %bitcast.93, ...), kind=kLoop, calls=%fused_computation.393 | loop fusion | flops 23855104 | bytes 4063356 | tf_op jit(solution)/shard_map/add | solution.py:48
  245.1 67.0 %all_to_all.16 = f32[128,16,128]{2,1,0:T(8,128)S(1)} all-to-all(f32[128,16,128]{2,1,0:T(8,128)S(1)} %gather_fusion.1), channel_id=1, replica_groups=mesh['view'=4,'brick'=128] {'brick'}, dimensions={0} | all-to-all | bytes 2097152 | tf_op jit(solution)/shard_map/all_to_all | solution.py:63
  313.2 58.4 %all-reduce.11.cloned.1.call-done = f32[1,2048,128]{2,1,0:T(8,128)} async-done(((f32[1,2048,128]{2,1,0:T(8,128)}), f32[1,2048,128]{2,1,0:T(8,128)}) %all-reduce.11.cloned.1.call-update) | async-done | bytes 1048592 | tf_op jit(solution)/shard_map/psum | solution.py:86
  373.0 66.2 %all_to_all.17 = f32[1,2048,128]{2,0,1:T(1,128)S(1)} all-to-all(f32[1,2048,128]{2,0,1:T(1,128)S(1)} %bitcast.119), channel_id=1, replica_groups=mesh['view'=4,'brick'=128] {'brick'}, dimensions={1} | all-to-all | bytes 2097152 | tf_op jit(solution)/shard_map/all_to_all | solution.py:53
  445.0 35.9 %collective-permute-done.4 = f32[128,15,128]{2,0,1:T(8,128)S(1)} collective-permute-done((f32[128,15,128]{2,0,1:T(8,128)S(1)}, f32[128,15,128]{2,0,1:T(8,128)S(1)}, u32[]{:S(2)}, u32[]{:S(2)}) %collective-permute-start.4) | collective-permute-done | bytes 983072 | tf_op jit(solution)/shard_map/ppermute | solution.py:14
  482.8 24.0 %fusion.155 = f32[128,16,128]{2,1,0:T(8,128)S(1)} fusion(f32[128,15,128]{2,1,0:T(8,128)S(1)} %copy.22, f32[128,16,128]{2,1,0:T(8,128)S(1)} %gather_fusion.2, f32[128,31,128]{2,1,0:T(8,128)S(1)} %copy_dynamic-update-slice_fusion, f32[]{:T(128)} %bitcast.44, f32[]{:T(128)} %bitcast.43, f32[]{:T(128)} %bitcast.42, f32[]{:T(128)} %bitcast.41, f32[]{:T(128)} %bitcast.40, ...), kind=kLoop, calls=%fused_computation.351 | loop fusion | flops 19922944 | bytes 18808956 | tf_op jit(solution)/shard_map/add | solution.py:48
  511.7 6.3 fusion.356
  522.9 6.1 fusion.44
  531.2 8.0 %collective-permute-start.6 = (f32[128,15,128]{2,0,1:T(8,128)S(1)}, f32[128,15,128]{2,0,1:T(8,128)S(1)}, u32[]{:S(2)}, u32[]{:S(2)}) collective-permute-start(f32[128,15,128]{2,0,1:T(8,128)S(1)} %copy.25), channel_id=1, source_target_pairs={{0,1},{1,2},{2,3},{3,4},{4,5},{5,6},{6,7},{7,8},{8,9},{9,10},{10,1... | collective-permute-start | bytes 2949128 | tf_op jit(solution)/shard_map/ppermute | solution.py:14
  539.2 16.0 %collective-permute-done.7 = f32[128,15,128]{2,0,1:T(8,128)S(1)} collective-permute-done((f32[128,15,128]{2,0,1:T(8,128)S(1)}, f32[128,15,128]{2,0,1:T(8,128)S(1)}, u32[]{:S(2)}, u32[]{:S(2)}) %collective-permute-start.7) | collective-permute-done | bytes 983072 | tf_op jit(solution)/shard_map/ppermute | solution.py:17
  555.8 24.8 %collective-permute-done.6 = f32[128,15,128]{2,0,1:T(8,128)S(1)} collective-permute-done((f32[128,15,128]{2,0,1:T(8,128)S(1)}, f32[128,15,128]{2,0,1:T(8,128)S(1)}, u32[]{:S(2)}, u32[]{:S(2)}) %collective-permute-start.6) | collective-permute-done | bytes 983072 | tf_op jit(solution)/shard_map/ppermute | solution.py:14
  582.2 31.2 %fusion.53 = f32[128,16,128]{2,1,0:T(8,128)S(1)} fusion(f32[128,16,128]{2,1,0:T(8,128)S(1)} %fusion.44, f32[128,15,128]{2,1,0:T(8,128)S(1)} %copy.28, f32[128,15,128]{2,1,0:T(8,128)} %copy.26, f32[]{:T(128)} %bitcast.98, f32[]{:T(128)} %bitcast.97, f32[]{:T(128)} %bitcast.96, f32[]{:T(128)} %bitcast.95, f32[]{:T(128)} %bitcast.94, f32[]{:T(128)} %bitcast.93, ...), kind=kLoop, calls=%fused_computation.249 | loop fusion | flops 23855104 | bytes 4063356 | tf_op jit(solution)/shard_map/add | solution.py:48
  614.2 64.9 %all_to_all.18 = f32[128,16,128]{2,1,0:T(8,128)S(1)} all-to-all(f32[128,16,128]{2,1,0:T(8,128)S(1)} %gather_fusion.3), channel_id=1, replica_groups=mesh['view'=4,'brick'=128] {'brick'}, dimensions={0} | all-to-all | bytes 2097152 | tf_op jit(solution)/shard_map/all_to_all | solution.py:63
  680.2 57.6 %all-reduce.13.cloned.1.call-done = f32[1,2048,128]{2,1,0:T(8,128)} async-done(((f32[1,2048,128]{2,1,0:T(8,128)}), f32[1,2048,128]{2,1,0:T(8,128)}) %all-reduce.13.cloned.1.call-update) | async-done | bytes 1048592 | tf_op jit(solution)/shard_map/psum | solution.py:86
  (83 shorter events, 59.9 us)
Async XLA Ops:
  6.5 21.6 %copy-start.4 = (f32[1,31]{1,0:T(1,128)S(1)}, f32[1,31]{1,0:T(1,128)}, u32[]{:S(2)}) copy-start(f32[1,31]{1,0:T(1,128)} %param.8) | copy-start | bytes 376
  6.5 22.3 %copy-start.3 = (f32[1,2,7]{2,1,0:T(2,128)S(1)}, f32[1,2,7]{2,1,0:T(2,128)}, u32[]{:S(2)}) copy-start(f32[1,2,7]{2,1,0:T(2,128)} %param.9) | copy-start | bytes 172
  6.5 23.2 %copy-start.6 = (s32[1,128]{1,0:T(1,128)S(1)}, s32[1,128]{1,0:T(1,128)}, u32[]{:S(2)}) copy-start(s32[1,128]{1,0:T(1,128)} %param.10) | copy-start | bytes 1540
  6.5 71.0 %all-to-all-start = ((f32[1,2048,128]{2,0,1:T(1,128)}), f32[1,2048,128]{2,0,1:T(1,128)S(1)}, u32[]{:S(2)}, u32[]{:S(2)}) async-start(f32[1,2048,128]{2,0,1:T(1,128)} %bitcast.120), calls=%async_computation | async-start | bytes 2097152 | tf_op jit(solution)/shard_map/all_to_all | solution.py:53
  28.1 343.5 %all-reduce.11.cloned.1.call-start = ((), (), s32[]{:S(2)}) async-start(), calls=%async_computation.4 | async-start | bytes 2097152 | tf_op jit(solution)/shard_map/psum | solution.py:86
  78.4 7.8 %copy-start.5 = (s32[1,128]{1,0:T(1,128)S(1)}, s32[1,128]{1,0:T(1,128)}, u32[]{:S(2)}) copy-start(s32[1,128]{1,0:T(1,128)} %param.11) | copy-start | bytes 1540
  79.1 40.7 %collective-permute-start = (f32[128,15,128]{2,0,1:T(8,128)S(1)}, f32[128,15,128]{2,0,1:T(8,128)S(1)}, u32[]{:S(2)}, u32[]{:S(2)}) collective-permute-start(f32[128,15,128]{2,0,1:T(8,128)S(1)} %copy.12), channel_id=1, source_target_pairs={{0,1},{1,2},{2,3},{3,4},{4,5},{5,6},{6,7},{7,8},{8,9},{9,10},{10,1... | collective-permute-start | bytes 2949128 | tf_op jit(solution)/shard_map/ppermute | solution.py:14
  82.1 38.3 %collective-permute-start.1 = (f32[128,15,128]{2,0,1:T(8,128)S(1)}, f32[128,15,128]{2,0,1:T(8,128)S(1)}, u32[]{:S(2)}, u32[]{:S(2)}) collective-permute-start(f32[128,15,128]{2,0,1:T(8,128)S(1)} %copy.14), channel_id=1, source_target_pairs={{1,0},{2,1},{3,2},{4,3},{5,4},{6,5},{7,6},{8,7},{9,8},{10,9},{11,1... | collective-permute-start | bytes 2949128 | tf_op jit(solution)/shard_map/ppermute | solution.py:17
  145.0 4.9 copy-start.1
  168.6 22.1 %collective-permute-start.3 = (f32[128,15,128]{2,0,1:T(8,128)}, f32[128,15,128]{2,0,1:T(8,128)}, u32[]{:S(2)}, u32[]{:S(2)}) collective-permute-start(f32[128,15,128]{2,0,1:T(8,128)} %copy.18), channel_id=1, source_target_pairs={{1,0},{2,1},{3,2},{4,3},{5,4},{6,5},{7,6},{8,7},{9,8},{10,9},{11,1... | collective-permute-start | bytes 2949128 | tf_op jit(solution)/shard_map/ppermute | solution.py:17
  171.2 47.3 %collective-permute-start.2 = (f32[128,15,128]{2,0,1:T(8,128)}, f32[128,15,128]{2,0,1:T(8,128)S(1)}, u32[]{:S(2)}, u32[]{:S(2)}) collective-permute-start(f32[128,15,128]{2,0,1:T(8,128)} %copy.16), channel_id=1, source_target_pairs={{0,1},{1,2},{2,3},{3,4},{4,5},{5,6},{6,7},{7,8},{8,9},{9,10},{10,1... | collective-permute-start | bytes 2949128 | tf_op jit(solution)/shard_map/ppermute | solution.py:14
  312.0 59.6 %copy-start = (f32[1,2048,128]{2,1,0:T(8,128)S(1)}, f32[1,2048,128]{2,1,0:T(8,128)}, u32[]{:S(2)}) copy-start(f32[1,2048,128]{2,1,0:T(8,128)} %param.6) | copy-start | bytes 3145732
  313.2 424.6 %all-reduce.13.cloned.1.call-start = ((), (), s32[]{:S(2)}) async-start(), calls=%async_computation.5 | async-start | bytes 2097152 | tf_op jit(solution)/shard_map/psum | solution.py:86
  440.5 40.4 %collective-permute-start.4 = (f32[128,15,128]{2,0,1:T(8,128)S(1)}, f32[128,15,128]{2,0,1:T(8,128)S(1)}, u32[]{:S(2)}, u32[]{:S(2)}) collective-permute-start(f32[128,15,128]{2,0,1:T(8,128)S(1)} %copy.21), channel_id=1, source_target_pairs={{0,1},{1,2},{2,3},{3,4},{4,5},{5,6},{6,7},{7,8},{8,9},{9,10},{10,1... | collective-permute-start | bytes 2949128 | tf_op jit(solution)/shard_map/ppermute | solution.py:14
  443.3 38.9 %collective-permute-start.5 = (f32[128,15,128]{2,0,1:T(8,128)S(1)}, f32[128,15,128]{2,0,1:T(8,128)S(1)}, u32[]{:S(2)}, u32[]{:S(2)}) collective-permute-start(f32[128,15,128]{2,0,1:T(8,128)S(1)} %copy.23), channel_id=1, source_target_pairs={{1,0},{2,1},{3,2},{4,3},{5,4},{6,5},{7,6},{8,7},{9,8},{10,9},{11,1... | collective-permute-start | bytes 2949128 | tf_op jit(solution)/shard_map/ppermute | solution.py:17
  506.8 4.9 copy-start.2
  529.6 25.7 %collective-permute-start.7 = (f32[128,15,128]{2,0,1:T(8,128)S(1)}, f32[128,15,128]{2,0,1:T(8,128)S(1)}, u32[]{:S(2)}, u32[]{:S(2)}) collective-permute-start(f32[128,15,128]{2,0,1:T(8,128)S(1)} %copy.27), channel_id=1, source_target_pairs={{1,0},{2,1},{3,2},{4,3},{5,4},{6,5},{7,6},{8,7},{9,8},{10,9},{11,1... | collective-permute-start | bytes 2949128 | tf_op jit(solution)/shard_map/ppermute | solution.py:17
  531.2 49.5 %collective-permute-start.6 = (f32[128,15,128]{2,0,1:T(8,128)S(1)}, f32[128,15,128]{2,0,1:T(8,128)S(1)}, u32[]{:S(2)}, u32[]{:S(2)}) collective-permute-start(f32[128,15,128]{2,0,1:T(8,128)S(1)} %copy.25), channel_id=1, source_target_pairs={{0,1},{1,2},{2,3},{3,4},{4,5},{5,6},{6,7},{7,8},{8,9},{9,10},{10,1... | collective-permute-start | bytes 2949128 | tf_op jit(solution)/shard_map/ppermute | solution.py:14
Sparse Core Ops, SparseCore 0:
  313.3 58.3 all-reduce.10
  680.3 57.4 all-reduce.12
where the time goes:
time: 749 us; the launch traced here: 747 us
  waiting for transfers between devices  306 us (41%)
  blocking collectives  198 us (26%)
  other arithmetic  159 us (21%)
  starting transfers between devices  46.5 us (6%)
  local copies, waits for them, and re-layouts  23.3 us (3%)
  between operations  13.8 us (2%)
    all_to_all x2, blocking collectives, to_reference(): lax.all_to_all(ordered, 'brick', split_axis=0, concat_axis=1, tiled=True)  132 us
    ppermute x4, waiting for transfers between devices, with_halo(): lax.ppermute(lax.slice_in_dim(block, block.shape[dim] - width, None, axis...  120 us
    psum x2, waiting for transfers between devices, on_device(): current = current * jnp.exp(lax.psum(log_terms, 'view'))  116 us
    add x4, other arithmetic, blur_rows(): summed + kernel[offset] * lax.slice_in_dim(padded, offset, offset + lengt...  104 us
    all_to_all x1, blocking collectives, to_view(): lax.all_to_all(volume, 'brick', split_axis=1, concat_axis=0, tiled=True)  66.2 us
    all_to_all x1, waiting for transfers between devices, to_view(): lax.all_to_all(volume, 'brick', split_axis=1, concat_axis=0, tiled=True)  43.9 us
    add x6, other arithmetic, blur_axis(): summed + kernel[offset] * lax.slice_in_dim(padded, offset, offset + lengt...  31.8 us
    ppermute x4, waiting for transfers between devices, with_halo(): lax.ppermute(lax.slice_in_dim(block, 0, width, axis=dim), axis, backward)  26.4 us
  transfers between devices with their start and end apart: 11, of which 10 were waited for; matrix products, arithmetic and copies ran while one was open for 2% of the time, Pallas kernels for 0%

commit v1 on v0

--- a/solution.py
+++ b/solution.py
@@ -50,7 +50,10 @@
 
 
 def to_view(volume, forward_map):
-    arrived = lax.all_to_all(volume, "brick", split_axis=1, concat_axis=0, tiled=True)
+    arrived = jnp.concatenate(
+        lax.all_to_all(jnp.stack(jnp.split(volume, lax.axis_size("brick"), axis=1)), "brick", 0, 0),
+        axis=0,
+    )
     brick_count = forward_map.shape[0]
     bricks = arrived.reshape(brick_count, -1, arrived.shape[1], arrived.shape[2])
     return bricks[forward_map].reshape(arrived.shape)

time: 749 us -> 929 us (1.24); the launches traced: 747 us -> 915 us
  local copies, waits for them, and re-layouts: 23.3 us -> 188 us
    unnamed x16 -> x270, local copies, waits for them, and re-layouts: 0.33 us -> 165 us
where the time goes in v1:
time: 929 us; the launch traced here: 915 us
  waiting for transfers between devices  308 us (33%)
  blocking collectives  198 us (21%)
  local copies, waits for them, and re-layouts  188 us (20%)
  other arithmetic  159 us (17%)
  starting transfers between devices  47 us (5%)
  between operations  15.3 us (2%)
    unnamed x270, local copies, waits for them, and re-layouts  165 us
    all_to_all x2, blocking collectives, to_reference(): lax.all_to_all(ordered, 'brick', split_axis=0, concat_axis=1, tiled=True)  131 us
    ppermute x4, waiting for transfers between devices, with_halo(): lax.ppermute(lax.slice_in_dim(block, block.shape[dim] - width, None, axis...  122 us
    psum x2, waiting for transfers between devices, on_device(): current = current * jnp.exp(lax.psum(log_terms, 'view'))  116 us
    add x4, other arithmetic, blur_rows(): summed + kernel[offset] * lax.slice_in_dim(padded, offset, offset + lengt...  105 us
    all_to_all x1, blocking collectives, to_view(): lax.all_to_all(jnp.stack(jnp.split(volume, lax.axis_size('brick'), axis=1...  66.2 us
    all_to_all x1, waiting for transfers between devices, to_view(): lax.all_to_all(jnp.stack(jnp.split(volume, lax.axis_size('brick'), axis=1...  43.9 us
    add x6, other arithmetic, blur_axis(): summed + kernel[offset] * lax.slice_in_dim(padded, offset, offset + lengt...  31.2 us
  transfers between devices with their start and end apart: 11, of which 10 were waited for; matrix products, arithmetic and copies ran while one was open for 2% of the time, Pallas kernels for 0%

profile of v1, /device:TPU:1, one launch (start us, length us, event | category | flops | bytes accessed | tf_op | source)
XLA Modules:
  0.0 915.2 jit_solution(16312308264970617379)
XLA Ops:
  172.4 21.4 %all-to-all-start = ((f32[128,1,16,128]{3,2,1,0:T(8,128)}), f32[128,1,16,128]{3,2,1,0:T(8,128)S(1)}, u32[]{:S(2)}, u32[]{:S(2)}) async-start(f32[128,1,16,128]{3,2,1,0:T(8,128)} %constant_dynamic-update-slice_fusion), calls=%async_computation | async-start | bytes 2097152 | tf_op jit(solution)/shard_map/all_to_all | solution.py:54
  199.3 43.9 %all-to-all-done = f32[128,1,16,128]{3,2,1,0:T(8,128)S(1)} async-done(((f32[128,1,16,128]{3,2,1,0:T(8,128)}), f32[128,1,16,128]{3,2,1,0:T(8,128)S(1)}, u32[]{:S(2)}, u32[]{:S(2)}) %all-to-all-start) | async-done | bytes 1048608 | tf_op jit(solution)/shard_map/all_to_all | solution.py:54
  252.3 33.3 %collective-permute-done = f32[128,15,128]{2,0,1:T(8,128)S(1)} collective-permute-done((f32[128,15,128]{2,0,1:T(8,128)S(1)}, f32[128,15,128]{2,0,1:T(8,128)S(1)}, u32[]{:S(2)}, u32[]{:S(2)}) %collective-permute-start) | collective-permute-done | bytes 983072 | tf_op jit(solution)/shard_map/ppermute | solution.py:14
  286.7 24.5 %fusion.299 = f32[128,16,128]{2,1,0:T(8,128)S(1)} fusion(f32[128,15,128]{2,1,0:T(8,128)S(1)} %copy.152, f32[128,16,128]{2,1,0:T(8,128)S(1)} %gather_fusion, f32[128,31,128]{2,1,0:T(8,128)S(1)} %copy_dynamic-update-slice_fusion.1, f32[]{:T(128)} %bitcast.171, f32[]{:T(128)} %bitcast.170, f32[]{:T(128)} %bitcast.169, f32[]{:T(128)} %bitcast.168, ...), kind=kLoop, calls=%fused_computation.495 | loop fusion | flops 19922944 | bytes 18808956 | tf_op jit(solution)/shard_map/add | solution.py:48
  316.2 6.5 fusion.357
  327.3 6.0 fusion.19
  336.3 6.6 collective-permute-start.2
  346.9 8.7 collective-permute-done.3
  356.2 27.6 %collective-permute-done.2 = f32[128,15,128]{2,0,1:T(8,128)} collective-permute-done((f32[128,15,128]{2,0,1:T(8,128)}, f32[128,15,128]{2,0,1:T(8,128)}, u32[]{:S(2)}, u32[]{:S(2)}) %collective-permute-start.2) | collective-permute-done | bytes 983072 | tf_op jit(solution)/shard_map/ppermute | solution.py:14
  385.6 25.0 %fusion.197 = f32[128,16,128]{2,1,0:T(8,128)S(1)} fusion(f32[128,16,128]{2,1,0:T(8,128)S(1)} %fusion.19, f32[128,15,128]{2,1,0:T(8,128)S(1)} %copy.158, f32[128,15,128]{2,1,0:T(8,128)S(1)} %copy.156, f32[]{:T(128)} %bitcast.225, f32[]{:T(128)} %bitcast.224, f32[]{:T(128)} %bitcast.223, f32[]{:T(128)} %bitcast.222, f32[]{:T(128)} %bitcast.221, f32[]{:T(128)} %bitcast.220, ...), kind=kLoop, calls=%fused_computation.393 | loop fusion | flops 23855104 | bytes 4063356 | tf_op jit(solution)/shard_map/add | solution.py:48
  411.4 66.4 %all_to_all.28 = f32[128,16,128]{2,1,0:T(8,128)S(1)} all-to-all(f32[128,16,128]{2,1,0:T(8,128)S(1)} %gather_fusion.1), channel_id=1, replica_groups=mesh['view'=4,'brick'=128] {'brick'}, dimensions={0} | all-to-all | bytes 2097152 | tf_op jit(solution)/shard_map/all_to_all | solution.py:66
  479.0 58.7 %all-reduce.11.cloned.1.call-done = f32[1,2048,128]{2,1,0:T(8,128)} async-done(((f32[1,2048,128]{2,1,0:T(8,128)}), f32[1,2048,128]{2,1,0:T(8,128)}) %all-reduce.11.cloned.1.call-update) | async-done | bytes 1048592 | tf_op jit(solution)/shard_map/psum | solution.py:89
  540.5 66.2 %all_to_all.29 = f32[128,1,16,128]{3,2,1,0:T(8,128)S(1)} all-to-all(f32[128,1,16,128]{3,2,1,0:T(8,128)S(1)} %constant_dynamic-update-slice_fusion.129), channel_id=1, replica_groups=mesh['view'=4,'brick'=128] {'brick'}, dimensions={0} | all-to-all | bytes 2097152 | tf_op jit(solution)/shard_map/all_to_all | solution.py:54
  612.3 36.1 %collective-permute-done.4 = f32[128,15,128]{2,0,1:T(8,128)S(1)} collective-permute-done((f32[128,15,128]{2,0,1:T(8,128)S(1)}, f32[128,15,128]{2,0,1:T(8,128)S(1)}, u32[]{:S(2)}, u32[]{:S(2)}) %collective-permute-start.4) | collective-permute-done | bytes 983072 | tf_op jit(solution)/shard_map/ppermute | solution.py:14
  650.3 24.5 %fusion.155 = f32[128,16,128]{2,1,0:T(8,128)S(1)} fusion(f32[128,15,128]{2,1,0:T(8,128)S(1)} %copy.160, f32[128,16,128]{2,1,0:T(8,128)S(1)} %gather_fusion.2, f32[128,31,128]{2,1,0:T(8,128)S(1)} %copy_dynamic-update-slice_fusion, f32[]{:T(128)} %bitcast.171, f32[]{:T(128)} %bitcast.170, f32[]{:T(128)} %bitcast.169, f32[]{:T(128)} %bitcast.168, ...), kind=kLoop, calls=%fused_computation.351 | loop fusion | flops 19922944 | bytes 18808956 | tf_op jit(solution)/shard_map/add | solution.py:48
  674.8 5.0 multiply_add_fusion.1
  679.8 6.5 fusion.356
  691.0 6.0 fusion.44
  699.1 8.0 collective-permute-start.6
  707.1 16.0 %collective-permute-done.7 = f32[128,15,128]{2,0,1:T(8,128)S(1)} collective-permute-done((f32[128,15,128]{2,0,1:T(8,128)S(1)}, f32[128,15,128]{2,0,1:T(8,128)S(1)}, u32[]{:S(2)}, u32[]{:S(2)}) %collective-permute-start.7) | collective-permute-done | bytes 983072 | tf_op jit(solution)/shard_map/ppermute | solution.py:17
  723.7 24.8 %collective-permute-done.6 = f32[128,15,128]{2,0,1:T(8,128)S(1)} collective-permute-done((f32[128,15,128]{2,0,1:T(8,128)S(1)}, f32[128,15,128]{2,0,1:T(8,128)S(1)}, u32[]{:S(2)}, u32[]{:S(2)}) %collective-permute-start.6) | collective-permute-done | bytes 983072 | tf_op jit(solution)/shard_map/ppermute | solution.py:14
  750.1 31.2 %fusion.53 = f32[128,16,128]{2,1,0:T(8,128)S(1)} fusion(f32[128,16,128]{2,1,0:T(8,128)S(1)} %fusion.44, f32[128,15,128]{2,1,0:T(8,128)S(1)} %copy.166, f32[128,15,128]{2,1,0:T(8,128)} %copy.164, f32[]{:T(128)} %bitcast.225, f32[]{:T(128)} %bitcast.224, f32[]{:T(128)} %bitcast.223, f32[]{:T(128)} %bitcast.222, f32[]{:T(128)} %bitcast.221, f32[]{:T(128)} %bitcast.220, ...), kind=kLoop, calls=%fused_computation.249 | loop fusion | flops 23855104 | bytes 4063356 | tf_op jit(solution)/shard_map/add | solution.py:48
  782.0 64.9 %all_to_all.30 = f32[128,16,128]{2,1,0:T(8,128)S(1)} all-to-all(f32[128,16,128]{2,1,0:T(8,128)S(1)} %gather_fusion.3), channel_id=1, replica_groups=mesh['view'=4,'brick'=128] {'brick'}, dimensions={0} | all-to-all | bytes 2097152 | tf_op jit(solution)/shard_map/all_to_all | solution.py:66
  848.0 57.6 %all-reduce.13.cloned.1.call-done = f32[1,2048,128]{2,1,0:T(8,128)} async-done(((f32[1,2048,128]{2,1,0:T(8,128)}), f32[1,2048,128]{2,1,0:T(8,128)}) %all-reduce.13.cloned.1.call-update) | async-done | bytes 1048592 | tf_op jit(solution)/shard_map/psum | solution.py:89
  (339 shorter events, 224.5 us)
Async XLA Ops:
  6.5 187.3 %copy-start.4 = (f32[1,31]{1,0:T(1,128)S(1)}, f32[1,31]{1,0:T(1,128)}, u32[]{:S(2)}) copy-start(f32[1,31]{1,0:T(1,128)} %param.8) | copy-start | bytes 376
  7.8 186.8 %copy-start.3 = (f32[1,2,7]{2,1,0:T(2,128)S(1)}, f32[1,2,7]{2,1,0:T(2,128)}, u32[]{:S(2)}) copy-start(f32[1,2,7]{2,1,0:T(2,128)} %param.9) | copy-start | bytes 172
  7.8 187.6 %copy-start.6 = (s32[1,128]{1,0:T(1,128)S(1)}, s32[1,128]{1,0:T(1,128)}, u32[]{:S(2)}) copy-start(s32[1,128]{1,0:T(1,128)} %param.10) | copy-start | bytes 1540
  172.4 70.8 %all-to-all-start = ((f32[128,1,16,128]{3,2,1,0:T(8,128)}), f32[128,1,16,128]{3,2,1,0:T(8,128)S(1)}, u32[]{:S(2)}, u32[]{:S(2)}) async-start(f32[128,1,16,128]{3,2,1,0:T(8,128)} %constant_dynamic-update-slice_fusion), calls=%async_computation | async-start | bytes 2097152 | tf_op jit(solution)/shard_map/all_to_all | solution.py:54
  193.8 343.9 %all-reduce.11.cloned.1.call-start = ((), (), s32[]{:S(2)}) async-start(), calls=%async_computation.4 | async-start | bytes 2097152 | tf_op jit(solution)/shard_map/psum | solution.py:89
  244.1 7.9 copy-start.5
  244.8 40.7 %collective-permute-start = (f32[128,15,128]{2,0,1:T(8,128)S(1)}, f32[128,15,128]{2,0,1:T(8,128)S(1)}, u32[]{:S(2)}, u32[]{:S(2)}) collective-permute-start(f32[128,15,128]{2,0,1:T(8,128)S(1)} %copy.151), channel_id=1, source_target_pairs={{0,1},{1,2},{2,3},{3,4},{4,5},{5,6},{6,7},{7,8},{8,9},{9,10},{10,1... | collective-permute-start | bytes 2949128 | tf_op jit(solution)/shard_map/ppermute | solution.py:14
  247.8 38.3 %collective-permute-start.1 = (f32[128,15,128]{2,0,1:T(8,128)S(1)}, f32[128,15,128]{2,0,1:T(8,128)S(1)}, u32[]{:S(2)}, u32[]{:S(2)}) collective-permute-start(f32[128,15,128]{2,0,1:T(8,128)S(1)} %copy.153), channel_id=1, source_target_pairs={{1,0},{2,1},{3,2},{4,3},{5,4},{6,5},{7,6},{8,7},{9,8},{10,9},{11,1... | collective-permute-start | bytes 2949128 | tf_op jit(solution)/shard_map/ppermute | solution.py:17
  311.2 5.0 copy-start.1
  333.8 21.8 %collective-permute-start.3 = (f32[128,15,128]{2,0,1:T(8,128)S(1)}, f32[128,15,128]{2,0,1:T(8,128)S(1)}, u32[]{:S(2)}, u32[]{:S(2)}) collective-permute-start(f32[128,15,128]{2,0,1:T(8,128)S(1)} %copy.157), channel_id=1, source_target_pairs={{1,0},{2,1},{3,2},{4,3},{5,4},{6,5},{7,6},{8,7},{9,8},{10,9},{11,1... | collective-permute-start | bytes 2949128 | tf_op jit(solution)/shard_map/ppermute | solution.py:17
  336.3 47.5 %collective-permute-start.2 = (f32[128,15,128]{2,0,1:T(8,128)}, f32[128,15,128]{2,0,1:T(8,128)}, u32[]{:S(2)}, u32[]{:S(2)}) collective-permute-start(f32[128,15,128]{2,0,1:T(8,128)} %copy.155), channel_id=1, source_target_pairs={{0,1},{1,2},{2,3},{3,4},{4,5},{5,6},{6,7},{7,8},{8,9},{9,10},{10,1... | collective-permute-start | bytes 2949128 | tf_op jit(solution)/shard_map/ppermute | solution.py:14
  477.8 59.9 %copy-start = (f32[1,2048,128]{2,1,0:T(8,128)S(1)}, f32[1,2048,128]{2,1,0:T(8,128)}, u32[]{:S(2)}) copy-start(f32[1,2048,128]{2,1,0:T(8,128)} %param.6) | copy-start | bytes 3145732
  479.0 426.6 %all-reduce.13.cloned.1.call-start = ((), (), s32[]{:S(2)}) async-start(), calls=%async_computation.5 | async-start | bytes 2097152 | tf_op jit(solution)/shard_map/psum | solution.py:89
  608.0 40.4 %collective-permute-start.4 = (f32[128,15,128]{2,0,1:T(8,128)S(1)}, f32[128,15,128]{2,0,1:T(8,128)S(1)}, u32[]{:S(2)}, u32[]{:S(2)}) collective-permute-start(f32[128,15,128]{2,0,1:T(8,128)S(1)} %copy.159), channel_id=1, source_target_pairs={{0,1},{1,2},{2,3},{3,4},{4,5},{5,6},{6,7},{7,8},{8,9},{9,10},{10,1... | collective-permute-start | bytes 2949128 | tf_op jit(solution)/shard_map/ppermute | solution.py:14
  610.8 38.9 %collective-permute-start.5 = (f32[128,15,128]{2,0,1:T(8,128)S(1)}, f32[128,15,128]{2,0,1:T(8,128)S(1)}, u32[]{:S(2)}, u32[]{:S(2)}) collective-permute-start(f32[128,15,128]{2,0,1:T(8,128)S(1)} %copy.161), channel_id=1, source_target_pairs={{1,0},{2,1},{3,2},{4,3},{5,4},{6,5},{7,6},{8,7},{9,8},{10,9},{11,1... | collective-permute-start | bytes 2949128 | tf_op jit(solution)/shard_map/ppermute | solution.py:17
  674.8 5.0 copy-start.2
  697.4 25.7 %collective-permute-start.7 = (f32[128,15,128]{2,0,1:T(8,128)S(1)}, f32[128,15,128]{2,0,1:T(8,128)S(1)}, u32[]{:S(2)}, u32[]{:S(2)}) collective-permute-start(f32[128,15,128]{2,0,1:T(8,128)S(1)} %copy.165), channel_id=1, source_target_pairs={{1,0},{2,1},{3,2},{4,3},{5,4},{6,5},{7,6},{8,7},{9,8},{10,9},{11,1... | collective-permute-start | bytes 2949128 | tf_op jit(solution)/shard_map/ppermute | solution.py:17
  699.1 49.5 %collective-permute-start.6 = (f32[128,15,128]{2,0,1:T(8,128)S(1)}, f32[128,15,128]{2,0,1:T(8,128)S(1)}, u32[]{:S(2)}, u32[]{:S(2)}) collective-permute-start(f32[128,15,128]{2,0,1:T(8,128)S(1)} %copy.163), channel_id=1, source_target_pairs={{0,1},{1,2},{2,3},{3,4},{4,5},{5,6},{6,7},{7,8},{8,9},{9,10},{10,1... | collective-permute-start | bytes 2949128 | tf_op jit(solution)/shard_map/ppermute | solution.py:14
Sparse Core Ops, SparseCore 0:
  479.1 58.5 all-reduce.10
  848.1 57.4 all-reduce.12
